TPU v7x, 32 devices: a whole 2x2x4 slice. The times are simulated.
32 devices in a mesh: dp: 8 (over z, x), seq: 4 (over y, core).
Axes of the slice: x: 2, y: 2, z: 4, core: 2. Of those that a mesh axis runs over, the one named last changes fastest.
Arguments:
- tokens: bfloat16 [8, 2048, 2048], P('dp', 'seq'), may hold values from -60 to 60
- in_gain: float32 [2048], replicated, may hold values from 0.1 to 1.9
- in_weight: bfloat16 [2048, 2304], P('dp'), may hold values from -0.125 to 0.125
- conv_weight: float32 [4, 2304], replicated, may hold values from -5 to 5
- conv_bias: float32 [2304], replicated, may hold values from -3 to 3
- log_decay: float32 [8, 32, 2048], P('dp', None, 'seq'), may hold values from -0.9 to 0
- skip: float32 [32], replicated, may hold values from 0.05 to 1
- out_gain: float32 [2048], replicated, may hold values from 0.1 to 1.9
- scan_order: int32 [512], replicated, may hold values from 0 to 511, each once
Outputs:
- regrouped: bfloat16 [8, 2048, 2048], P('dp', 'seq')
Inputs may be any that keep to these rules, and one draw needn't show every extreme that they name: Each of the 512 positions appears once; the q-th position of a frame in the next layer's scan is scan_order[q].
All inputs are finite; a program needn't handle non-finite values.
Results may differ from a plain program's by a relative error of at most 0.008.
Values may be sent and summed in bfloat16 or wider, within the bound.
A program may use at most 128 MiB of HBM per device.

v0:
```python
import jax
import jax.numpy as jnp
from jax import lax
from jax.sharding import PartitionSpec as P

HALF_HEADS = 32
HEADDIM = 64
STATE = 128
GROUP = 128
POSITIONS = 512


def passed_along(block, axis, distance):
    devices = range(lax.axis_size(axis))
    route = [(i - distance, i) for i in devices if i - distance in devices]
    return lax.ppermute(block, axis, route)


def entering_2(part, axis, combine, identity):
    place = lax.axis_index(axis)
    gathered = jax.tree.map(lambda a: lax.all_gather(a, axis), part)
    state = jax.tree.map(lambda a, e: jnp.zeros_like(a) + jnp.asarray(e, a.dtype), part, identity)

    def one(step, state):
        return combine(
            state, jax.tree.map(lambda a: lax.dynamic_index_in_dim(a, step, 0, False), gathered)
        )

    return lax.fori_loop(0, place, one, state)


def project(operand, in_weight, channels):
    seq_count = lax.axis_size("seq")
    slab_width = channels // seq_count
    column_slab = lax.dynamic_slice_in_dim(
        in_weight, lax.axis_index("seq") * slab_width, slab_width, 1
    )
    full_slab = lax.all_gather(column_slab, "dp", axis=0, tiled=True)
    return jnp.dot(
        operand,
        lax.all_gather(full_slab, "seq", axis=1, tiled=True),
        preferred_element_type=jnp.float32,
    ).astype(jnp.bfloat16)


def combine_states(earlier, later):
    return (earlier[0] * later[0], later[0][:, None, None] * earlier[1] + later[1])


def on_device(
    tokens, in_gain, in_weight, conv_weight, conv_bias, log_decay, skip, out_gain, scan_order
):
    own_tokens = tokens[0]
    token_count = own_tokens.shape[0]
    channels = in_weight.shape[1]
    tap_count = conv_weight.shape[0]
    margin = tap_count - 1
    widened = own_tokens.astype(jnp.float32)
    inverse = lax.rsqrt(jnp.mean(widened * widened, axis=1, keepdims=True) + 1e-05)
    normed = (widened * inverse * in_gain[None, :]).astype(jnp.bfloat16)
    projected = project(normed, in_weight, channels)
    earlier_rows = passed_along(projected[token_count - margin :], "seq", 1)
    extended = jnp.concatenate([earlier_rows, projected], axis=0)
    mixed_pre = conv_bias[None, :] + conv_weight[0][None, :] * extended[0:token_count].astype(
        jnp.float32
    )
    for offset in range(1, tap_count):
        mixed_pre = mixed_pre + conv_weight[offset][None, :] * extended[
            offset : offset + token_count
        ].astype(jnp.float32)
    mixed = jax.nn.silu(mixed_pre).astype(jnp.bfloat16)
    inner_width = HALF_HEADS * HEADDIM
    x_heads = mixed[:, :inner_width].reshape(token_count, HALF_HEADS, HEADDIM)
    b_vectors = mixed[:, inner_width : inner_width + STATE]
    c_vectors = mixed[:, inner_width + STATE :]
    own_decay = log_decay[0]
    block_count = token_count // GROUP
    places = jnp.arange(GROUP)
    causal = places[None, :] <= places[:, None]
    intra_parts = []
    block_states = []
    closings = []
    cumulatives = []
    device_state = jnp.zeros((HALF_HEADS, HEADDIM, STATE), jnp.float32)
    device_decay = jnp.ones((HALF_HEADS,), jnp.float32)
    for block_index in range(block_count):
        first_row = block_index * GROUP
        end_row = first_row + GROUP
        x_block = x_heads[first_row:end_row]
        b_block = b_vectors[first_row:end_row]
        c_block = c_vectors[first_row:end_row]
        decay_block = own_decay[:, first_row:end_row]
        cumulative = jnp.cumsum(decay_block, axis=1)
        step_size = -decay_block
        scores = lax.dot_general(
            c_block, b_block, (((1,), (1,)), ((), ())), preferred_element_type=jnp.float32
        )
        log_gap = cumulative[:, :, None] - cumulative[:, None, :]
        decay_mask = jnp.exp(jnp.where(causal[None], log_gap, -1e30))
        weights = (scores[None] * decay_mask * step_size[:, None, :]).astype(jnp.bfloat16)
        intra_parts.append(
            jnp.einsum("hts,shp->thp", weights, x_block, preferred_element_type=jnp.float32)
        )
        closing = cumulative[:, -1:]
        scaled = (
            (jnp.exp(closing - cumulative) * step_size).T[:, :, None] * x_block.astype(jnp.float32)
        ).astype(jnp.bfloat16)
        block_state = jnp.einsum("shp,sn->hpn", scaled, b_block, preferred_element_type=jnp.float32)
        fading = jnp.exp(closing[:, 0])
        device_state = fading[:, None, None] * device_state + block_state
        device_decay = device_decay * fading
        block_states.append(block_state)
        closings.append(fading)
        cumulatives.append(cumulative)
    carried = entering_2(
        (device_decay, device_state),
        "seq",
        combine_states,
        (jnp.ones_like(device_decay), jnp.zeros_like(device_state)),
    )
    entering = carried[1]
    outputs = []
    for block_index in range(block_count):
        first_row = block_index * GROUP
        c_block = c_vectors[first_row : first_row + GROUP]
        inter = jnp.einsum(
            "tn,hpn->thp",
            c_block,
            entering.astype(jnp.bfloat16),
            preferred_element_type=jnp.float32,
        )
        inter = inter * jnp.exp(cumulatives[block_index]).T[:, :, None]
        outputs.append(intra_parts[block_index] + inter)
        entering = closings[block_index][:, None, None] * entering + block_states[block_index]
    ssm_out = jnp.concatenate(outputs, axis=0) + skip[None, :, None] * x_heads.astype(jnp.float32)
    head_scale = lax.rsqrt(jnp.mean(ssm_out * ssm_out, axis=2, keepdims=True) + 1e-05)
    normalized = (ssm_out * head_scale * out_gain.reshape(HALF_HEADS, HEADDIM)[None]).astype(
        jnp.bfloat16
    )
    frames_here = token_count // POSITIONS
    framed = normalized.reshape(frames_here, POSITIONS, inner_width)
    picked = jnp.take(framed, scan_order, axis=1).transpose(1, 0, 2)
    seq_count = lax.axis_size("seq")
    outgoing = picked.reshape(seq_count, POSITIONS // seq_count, frames_here, inner_width)
    arrived = lax.all_to_all(outgoing, "seq", split_axis=0, concat_axis=2, tiled=True)
    return arrived.reshape(1, token_count, inner_width)


def solution(mesh):
    in_specs = (
        P("dp", "seq", None),
        P(),
        P("dp", None),
        P(),
        P(),
        P("dp", None, "seq"),
        P(),
        P(),
        P(),
    )
    out_specs = P("dp", "seq", None)
    return jax.shard_map(
        on_device, mesh=mesh, in_specs=in_specs, out_specs=out_specs, check_vma=False
    )
```

profile of v0, /device:TPU:25, one launch (start us, length us, event | category | flops | bytes accessed | tf_op | source)
XLA Modules:
  0.0 270.9 jit_solution(9146616953547675616)
XLA Ops:
  10.6 53.1 %all-gather.6.cloned.1.call-done = bf16[2048,576]{0,1:T(8,128)(2,1)} async-done(((bf16[256,576]{0,1:T(8,128)(2,1)}), bf16[2048,576]{0,1:T(8,128)(2,1)}) %all-gather.6.cloned.1.call-update) | async-done | bytes 2359312 | tf_op jit(solution)/shard_map/all_gather | solution.py:38
  67.5 62.4 %all-gather.8.cloned.1.call-done = bf16[2048,2304]{0,1:T(8,128)(2,1)} async-done(((bf16[2048,576]{0,1:T(8,128)(2,1)}), bf16[2048,2304]{0,1:T(8,128)(2,1)}) %all-gather.8.cloned.1.call-update) | async-done | bytes 9437200 | tf_op jit(solution)/shard_map/all_gather | solution.py:41
  129.9 9.1 %convolution_convert_fusion = bf16[512,2304]{1,0:T(8,128)(2,1)S(1)} fusion(bf16[2048,2304]{0,1:T(8,128)(2,1)} %all-gather.8.cloned.1.call-done, bf16[1,512,2048]{2,1,0:T(8,128)(2,1)S(1)} %copy-done.23, f32[2048]{0:T(1024)S(1)} %copy-done.45, f32[512]{0:T(512)S(1)} %add_rsqrt_fusion.1), kind=kOutput, calls=%fused_computation.6 | convolution fusion | flops 4837212160 | bytes 13903872 | tf_op jit(solution)/shard_map/dot_general | solution.py:39
  139.0 2.3 collective-permute-start
  143.1 3.4 %multiply_convert_fusion = bf16[512,2304]{1,0:T(8,128)(2,1)S(1)} fusion(bf16[512,2304]{1,0:T(8,128)(2,1)S(1)} %convolution_convert_fusion, bf16[3,2304]{1,0:T(4,128)(2,1)S(1)} %collective-permute-done, f32[2304]{0:T(1024)S(1)} %get-tuple-element.52, f32[2304]{0:T(1024)S(1)} %get-tuple-element.53, f32[2304]{0:T(1024)S(1)} %get-tuple-element.51, ...), kind=kLoop, calls=%fused_computation.5 | loop fusion | flops 30670848 | bytes 4778496 | tf_op jit(solution)/shard_map/convert_element_type | solution.py:71
  148.1 2.1 copy.48
  150.1 2.0 copy.49
  162.8 5.1 %all-reduce = f32[128]{0:T(128)S(1)} all-reduce(f32[128]{0:T(128)S(1)} %dynamic-update-slice), channel_id=2, replica_groups=mesh['dp'=8,'seq'=4] {'seq'}, use_global_device_ids=true, to_apply=%add | all-reduce | flops 128 | bytes 1024
  171.4 2.5 slice_convert_fusion
  173.9 5.5 %copy.56 = f32[512,2048]{0,1:T(8,128)} copy(f32[512,2048]{1,0:T(8,128)} %slice_convert_fusion) | data formatting | bytes 8388608 | tf_op jit(solution)/shard_map/convert_element_type | solution.py:135
  180.0 2.7 convolution_bitcast_fusion.3
  182.7 1.9 convolution_bitcast_fusion.2
  184.6 1.9 convolution_bitcast_fusion.1
  186.6 1.9 convolution_bitcast_fusion
  188.5 7.2 %all-gather.10.cloned.1.call-done = f32[128,64,128]{2,1,0:T(8,128)} async-done(((f32[32,64,128]{2,1,0:T(8,128)}), f32[128,64,128]{2,1,0:T(8,128)}) %all-gather.10.cloned.1.call-update) | async-done | bytes 4194320 | tf_op jit(solution)/shard_map/all_gather | solution.py:21
  195.8 2.3 while.12
  198.2 1.9 multiply_add_fusion
  207.0 2.5 mul.430
  209.5 5.5 %copy.57 = f32[512,2048]{1,0:T(8,128)} copy(f32[512,2048]{0,1:T(8,128)} %bitcast.92) | data formatting | bytes 8388608 | tf_op jit(solution)/shard_map/mul | solution.py:137
  220.3 4.6 %fusion.5 = bf16[512,2048]{1,0:T(8,128)(2,1)S(1)} fusion(f32[512,2048]{1,0:T(8,128)} %copy.57, f32[128,2048]{1,0:T(8,128)} %copy.55, f32[128,2048]{1,0:T(8,128)} %copy.54, f32[128,2048]{1,0:T(8,128)} %copy.53, f32[128,2048]{1,0:T(8,128)} %copy.52, f32[2048]{0:T(1024)S(1)} %copy-done.36, f32[2048]{0:T(1024)S(1)} %mul.424, bf16[512,2304]{1,0:T(8,128)(2,1)} %copy-done.2), kind=kLoop, calls=%fused_computation.13 | loop fusion | flops 9437184 | bytes 12599296 | tf_op jit(solution)/shard_map/convert_element_type | solution.py:137
  224.9 3.3 %gather_fusion = bf16[512,2048]{1,0:T(8,128)(2,1)} fusion(bf16[512,2048]{1,0:T(8,128)(2,1)S(1)} %fusion.5, s32[1024]{0:T(1024)S(1)} %pad_clamp_fusion), kind=kCustom, calls=%fused_computation | custom fusion | bytes 4196352 | tf_op jit(solution)/shard_map/jit(_take)/gather | solution.py:142
  228.2 1.8 broadcast_select_fusion
  230.0 30.7 %all_to_all.15 = bf16[4,128,1,2048]{3,1,2,0:T(8,128)(2,1)S(1)} all-to-all(bf16[4,128,1,2048]{3,1,2,0:T(8,128)(2,1)S(1)} %broadcast_select_fusion), channel_id=1, replica_groups=mesh['dp'=8,'seq'=4] {'seq'}, dimensions={0} | all-to-all | bytes 4194304 | tf_op jit(solution)/shard_map/all_to_all | solution.py:145
  262.4 2.0 reshape.199
  (151 shorter events, 41.1 us)
Async XLA Ops:
  6.5 57.2 %copy-start.28 = (f32[1,32,512]{2,1,0:T(8,128)S(1)}, f32[1,32,512]{2,1,0:T(8,128)}, u32[]{:S(2)}) copy-start(f32[1,32,512]{2,1,0:T(8,128)} %param.16) | copy-start | bytes 196612
  6.5 59.7 %copy-start.23 = (bf16[1,512,2048]{2,1,0:T(8,128)(2,1)S(1)}, bf16[1,512,2048]{2,1,0:T(8,128)(2,1)}, u32[]{:S(2)}) copy-start(bf16[1,512,2048]{2,1,0:T(8,128)(2,1)} %param.11) | copy-start | bytes 6291460
  6.5 57.2 %all-gather.6.cloned.1.call-start = ((), (), s32[]{:S(2)}) async-start(), calls=%async_computation.1 | async-start | bytes 2654208 | tf_op jit(solution)/shard_map/all_gather | solution.py:38
  10.5 119.3 %all-gather.8.cloned.1.call-start = ((), (), s32[]{:S(2)}) async-start(), calls=%async_computation.2 | async-start | bytes 11796480 | tf_op jit(solution)/shard_map/all_gather | solution.py:41
  63.7 66.2 %copy-start.45 = (f32[2048]{0:T(1024)S(1)}, f32[2048]{0:T(1024)}, u32[]{:S(2)}) copy-start(f32[2048]{0:T(1024)} %param.12) | copy-start | bytes 24580
  63.7 132.0 %all-gather.10.cloned.1.call-start = ((), (), s32[]{:S(2)}) async-start(), calls=%async_computation.3 | async-start | bytes 5242880 | tf_op jit(solution)/shard_map/all_gather | solution.py:21
  67.5 73.8 %copy-start.30 = (f32[4,2304]{1,0:T(4,128)S(1)}, f32[4,2304]{1,0:T(4,128)}, u32[]{:S(2)}) copy-start(f32[4,2304]{1,0:T(4,128)} %param.14) | copy-start | bytes 110596
  67.5 75.7 %copy-start.35 = (f32[2304]{0:T(1024)S(1)}, f32[2304]{0:T(1024)}, u32[]{:S(2)}) copy-start(f32[2304]{0:T(1024)} %param.15) | copy-start | bytes 27652
  139.0 4.2 %collective-permute-start = (bf16[3,2304]{1,0:T(4,128)(2,1)S(1)}, bf16[3,2304]{1,0:T(4,128)(2,1)S(1)}, u32[]{:S(2)}, u32[]{:S(2)}) collective-permute-start(bf16[3,2304]{1,0:T(4,128)(2,1)S(1)} %slice.152), channel_id=1, source_target_pairs={{0,1},{1,2},{2,3},{4,5},{5,6},{6,7},{8,9},{9,10},{10,11},{12,13},{... | collective-permute-start | bytes 41480 | tf_op jit(solution)/shard_map/ppermute | solution.py:16
  146.5 56.3 %copy-start.2 = (bf16[512,2304]{1,0:T(8,128)(2,1)}, bf16[512,2304]{1,0:T(8,128)(2,1)S(1)}, u32[]{:S(2)}) copy-start(bf16[512,2304]{1,0:T(8,128)(2,1)S(1)} %multiply_convert_fusion) | copy-start | bytes 7077892
  154.2 4.6 %copy-start.17 = (bf16[128,2048]{0,1:T(8,128)(2,1)S(1)}, bf16[128,2048]{0,1:T(8,128)(2,1)}, u32[]{:S(2)}) copy-start(bf16[128,2048]{0,1:T(8,128)(2,1)} %copy.51) | copy-start | bytes 1572868
  154.2 4.6 %copy-start.38 = (f32[32]{0:T(128)S(1)}, f32[32]{0:T(128)}, u32[]{:S(2)}) copy-start(f32[32]{0:T(128)} %exp.131) | copy-start | bytes 388
  154.2 4.6 %copy-start.40 = (f32[32]{0:T(128)S(1)}, f32[32]{0:T(128)}, u32[]{:S(2)}) copy-start(f32[32]{0:T(128)} %exp.132) | copy-start | bytes 388
  154.2 4.5 %copy-start.43 = (f32[32]{0:T(128)S(1)}, f32[32]{0:T(128)}, u32[]{:S(2)}) copy-start(f32[32]{0:T(128)} %get-tuple-element.90) | copy-start | bytes 388
  154.2 4.5 %copy-start.44 = (f32[32]{0:T(128)S(1)}, f32[32]{0:T(128)}, u32[]{:S(2)}) copy-start(f32[32]{0:T(128)} %exp.130) | copy-start | bytes 388
  155.7 4.5 %copy-start.3 = (f32[32,64,128]{2,1,0:T(8,128)}, f32[32,64,128]{2,1,0:T(8,128)S(1)}, u32[]{:S(2)}) copy-start(f32[32,64,128]{2,1,0:T(8,128)S(1)} %fusion.42) | copy-start | bytes 3145732
  173.9 6.0 %copy-start.22 = (bf16[128,2048]{0,1:T(8,128)(2,1)S(1)}, bf16[128,2048]{0,1:T(8,128)(2,1)}, u32[]{:S(2)}) copy-start(bf16[128,2048]{0,1:T(8,128)(2,1)} %copy.48) | copy-start | bytes 1572868
  179.4 3.3 %copy-start.21 = (bf16[128,2048]{0,1:T(8,128)(2,1)S(1)}, bf16[128,2048]{0,1:T(8,128)(2,1)}, u32[]{:S(2)}) copy-start(bf16[128,2048]{0,1:T(8,128)(2,1)} %copy.49) | copy-start | bytes 1572868
  179.4 3.3 %copy-start.33 = (f32[32,128]{1,0:T(8,128)S(1)}, f32[32,128]{1,0:T(8,128)}, u32[]{:S(2)}) copy-start(f32[32,128]{1,0:T(8,128)} %get-tuple-element.78) | copy-start | bytes 49156
  179.4 3.3 %copy-start.34 = (pred[128,128]{1,0:T(8,128)(4,1)S(1)}, pred[128,128]{1,0:T(8,128)(4,1)}, u32[]{:S(2)}) copy-start(pred[128,128]{1,0:T(8,128)(4,1)} %iota_compare_fusion) | copy-start | bytes 49156
  200.5 4.6 %copy-start.6 = (f32[128,32,64]{0,2,1:T(8,128)}, f32[128,32,64]{0,2,1:T(8,128)S(1)}, u32[]{:S(2)}) copy-start(f32[128,32,64]{0,2,1:T(8,128)S(1)} %fusion.17) | copy-start | bytes 3145732
  202.7 4.2 %copy-start.10 = (f32[128,32,64]{0,2,1:T(8,128)}, f32[128,32,64]{0,2,1:T(8,128)S(1)}, u32[]{:S(2)}) copy-start(f32[128,32,64]{0,2,1:T(8,128)S(1)} %fusion.15) | copy-start | bytes 3145732
  209.5 5.5 %copy-start.7 = (f32[128,32,64]{0,2,1:T(8,128)S(1)}, f32[128,32,64]{0,2,1:T(8,128)}, u32[]{:S(2)}) copy-start(f32[128,32,64]{0,2,1:T(8,128)} %copy-done.6) | copy-start | bytes 3145732
  260.7 3.6 %copy-start.1 = (bf16[256,2304]{1,0:T(8,128)(2,1)S(1)}, bf16[256,2304]{1,0:T(8,128)(2,1)}, u32[]{:S(2)}) copy-start(bf16[256,2304]{1,0:T(8,128)(2,1)} %param.13) | copy-start | bytes 3538948
  (26 other events, 55.3 us)
Sparse Core Ops, SparseCore 0:
  10.7 53.0 all-gather.5
  65.3 64.5 all-gather.7
  160.3 35.3 all-gather.9
where the time goes:
time: 274 us; the launch traced here: 271 us
  waiting for transfers between devices  123 us (45%)
  local copies, waits for them, and re-layouts  48.9 us (18%)
  blocking collectives  35.8 us (13%)
  matrix products  24.3 us (9%)
  other arithmetic  22.3 us (8%)
  between operations  14.2 us (5%)
    all_gather x1, waiting for transfers between devices, project(): lax.all_gather(full_slab, 'seq', axis=1, tiled=True)  62.4 us
    all_gather x1, waiting for transfers between devices, project(): full_slab = lax.all_gather(column_slab, 'dp', axis=0, tiled=True)  53.1 us
    all_to_all x1, blocking collectives, on_device(): lax.all_to_all(outgoing, 'seq', split_axis=0, concat_axis=2, tiled=True)  30.7 us
    unnamed x96, local copies, waits for them, and re-layouts  10.7 us
    dot_general x1, matrix products, project(): jnp.dot(operand, lax.all_gather(full_slab, 'seq', axis=1, tiled=True), pr...  9.08 us
    dot_general x4, matrix products, on_device(): jnp.einsum('hts,shp->thp', weights, x_block, preferred_element_type=jnp.f...  8.47 us
    mul x2, local copies, waits for them, and re-layouts, on_device(): ssm_out * head_scale * out_gain.reshape(HALF_HEADS, HEADDIM)[None]  7.96 us
    slice x5, local copies, waits for them, and re-layouts, on_device(): x_block = x_heads[first_row:end_row]  7.66 us
  transfers between devices with their start and end apart: 4, of which 3 were waited for; matrix products, arithmetic and copies ran while one was open for 10% of the time, Pallas kernels for 0%

commit v1 on v0

v1 whole, which is shorter than its diff:
```python
import functools
import math

import jax
import jax.numpy as jnp
from jax import lax
from jax.experimental import pallas as pl
from jax.experimental.pallas import tpu as pltpu
from jax.sharding import PartitionSpec as P

GROUP = 128
CHUNK = 256
HALO = 16
BF16 = jnp.bfloat16
F32 = jnp.float32
MESH = pl.DeviceIdType.MESH


def fused_kernel(
    sizes,
    tokens_ref,
    gain_ref,
    weight_ref,
    conv_weight_ref,
    conv_bias_ref,
    decay_ref,
    lane_ref,
    order_ref,
    result_ref,
    slabs,
    normed,
    projected,
    mixed,
    b_turned,
    c_held,
    scores,
    block_states,
    entering_half,
    intra,
    expanded,
    arriving_state,
    leaving_state,
    normalized,
    picked,
    z_send,
    z_recv,
    x_send,
    x_recv,
    core_send,
    core_recv,
    halo_send,
    halo_recv,
    state_send,
    state_recv,
    out_send,
    out_recv,
    own_sem,
):
    z_count, x_count, core_count, seq_count, head_width = sizes
    head_count = CHUNK // head_width
    dp = lax.axis_index("dp")
    seq = lax.axis_index("seq")
    z = dp // x_count
    x = dp % x_count
    core = seq % core_count
    sibling = seq - core + (core + 1) % core_count
    half = slabs.shape[4]
    slab_count = slabs.shape[0]
    chunk_count = slab_count - 1
    token_count, width = tokens_ref.shape
    block_count = token_count // GROUP
    positions = order_ref.shape[0]
    share = positions // seq_count

    partners = [(((z + k) % z_count) * x_count + x, seq) for k in range(1, z_count)]
    partners += [(z * x_count + (x + k) % x_count, seq) for k in range(1, x_count)]
    partners += [(dp, (seq + k) % seq_count) for k in range(1, seq_count)]
    barrier = pltpu.get_barrier_semaphore()
    for partner in partners:
        pl.semaphore_signal(barrier, inc=1, device_id=partner, device_id_type=MESH)

    own_rows = pl.ds(pl.multiple_of(core * half, half), half)
    for slab in range(slab_count):
        first = chunk_count * CHUNK if slab == 0 else (slab - 1) * CHUNK
        slabs[slab, z, x, core] = weight_ref[own_rows, first : first + CHUNK]
    pl.semaphore_wait(barrier, len(partners))

    def z_copy(slab, k, source):
        return pltpu.make_async_remote_copy(
            src_ref=slabs.at[slab, source, x, core],
            dst_ref=slabs.at[slab, source, x, core],
            send_sem=z_send.at[slab, k - 1],
            recv_sem=z_recv.at[slab, k - 1],
            device_id=(((z + k) % z_count) * x_count + x, seq),
            device_id_type=MESH,
        )

    def x_copy(slab, k, source):
        return pltpu.make_async_remote_copy(
            src_ref=slabs.at[slab, :, source, core],
            dst_ref=slabs.at[slab, :, source, core],
            send_sem=x_send.at[slab, k - 1],
            recv_sem=x_recv.at[slab, k - 1],
            device_id=(z * x_count + (x + k) % x_count, seq),
            device_id_type=MESH,
        )

    def core_copy(slab, source):
        return pltpu.make_async_remote_copy(
            src_ref=slabs.at[slab, :, :, source],
            dst_ref=slabs.at[slab, :, :, source],
            send_sem=core_send.at[slab],
            recv_sem=core_recv.at[slab],
            device_id=(dp, sibling),
            device_id_type=MESH,
        )

    for slab in range(slab_count):
        for k in range(1, z_count):
            z_copy(slab, k, z).start()

    def pass_x(slab):
        for k in range(1, z_count):
            z_copy(slab, k, (z + z_count - k) % z_count).wait_recv()
        for k in range(1, x_count):
            x_copy(slab, k, x).start()

    def pass_core(slab):
        for k in range(1, x_count):
            x_copy(slab, k, (x + x_count - k) % x_count).wait_recv()
        if core_count > 1:
            core_copy(slab, core).start()

    def whole_slab(slab):
        if core_count > 1:
            core_copy(slab, (core + 1) % core_count).wait_recv()

    for block in range(block_count):
        rows = tokens_ref[block * GROUP : (block + 1) * GROUP, :].astype(F32)
        inverse = lax.rsqrt(jnp.mean(rows * rows, axis=1, keepdims=True) + 1e-05)
        normed[HALO + block * GROUP : HALO + (block + 1) * GROUP, :] = (
            rows * inverse * gain_ref[...]
        ).astype(BF16)

    halo_copy = pltpu.make_async_remote_copy(
        src_ref=normed.at[token_count : token_count + HALO],
        dst_ref=normed.at[0:HALO],
        send_sem=halo_send,
        recv_sem=halo_recv,
        device_id=(dp, (seq + 1) % seq_count),
        device_id_type=MESH,
    )

    @pl.when(seq < seq_count - 1)
    def _():
        halo_copy.start()

    @pl.when(seq == 0)
    def _():
        normed[0:HALO, :] = jnp.zeros((HALO, width), BF16)

    row_at = lax.broadcasted_iota(jnp.int32, (GROUP, GROUP), 0)
    column_at = lax.broadcasted_iota(jnp.int32, (GROUP, GROUP), 1)
    causal = column_at <= row_at
    lower = jnp.where(causal, 1.0, 0.0).astype(F32)
    unit = jnp.where(row_at == column_at, 1.0, 0.0).astype(F32)
    upper = jnp.where(row_at <= column_at, 1.0, 0.0).astype(F32)
    first_head = lax.broadcasted_iota(jnp.int32, (1, GROUP), 1) < head_width
    same_head = jnp.where(row_at // head_width == column_at // head_width, 1.0, 0.0).astype(BF16)
    same_head_twice = jnp.concatenate([same_head, same_head], axis=0)

    def project(slab):
        matrix = slabs[slab].reshape(width, CHUNK)
        projected[...] = (
            jnp.dot(normed[...], matrix, preferred_element_type=F32).astype(BF16).astype(F32)
        )
        taps = conv_weight_ref.shape[1]
        for block in range(block_count):
            total = conv_bias_ref[slab]
            for tap in range(taps):
                first = HALO + block * GROUP + tap - (taps - 1)
                total = total + conv_weight_ref[slab, tap : tap + 1, :] * projected[
                    first : first + GROUP, :
                ]
            mixed[block * GROUP : (block + 1) * GROUP, :] = (total / (1.0 + jnp.exp(-total))).astype(
                BF16
            )

    def both(columns, pair):
        return jnp.where(
            first_head, columns[:, 2 * pair : 2 * pair + 1], columns[:, 2 * pair + 1 : 2 * pair + 2]
        )

    pass_x(0)
    pass_x(1)
    pass_core(0)

    @pl.when(seq > 0)
    def _():
        halo_copy.wait_recv()

    whole_slab(0)
    project(0)
    for block in range(block_count):
        rows = slice(block * GROUP, (block + 1) * GROUP)
        b_block = mixed[rows, :GROUP]
        c_block = mixed[rows, GROUP:]
        c_held[block] = c_block
        b_turned[block] = jnp.transpose(b_block.astype(F32)).astype(BF16)
        scores[block] = jnp.where(
            causal, jnp.dot(c_block, b_turned[block], preferred_element_type=F32), 0.0
        )
    order = order_ref[...]
    choice = jnp.where(
        lax.broadcasted_iota(jnp.int32, (positions, positions), 1) == order, 1.0, 0.0
    ).astype(BF16)

    def state_copy(chunk):
        return pltpu.make_async_remote_copy(
            src_ref=leaving_state.at[chunk],
            dst_ref=arriving_state.at[chunk],
            send_sem=state_send.at[chunk],
            recv_sem=state_recv.at[chunk],
            device_id=(dp, (seq + 1) % seq_count),
            device_id_type=MESH,
        )

    def out_columns(chunk):
        return pl.ds(pl.multiple_of(chunk * CHUNK, CHUNK), CHUNK)

    def work(chunk, carry):
        slab = chunk + 1

        @pl.when(slab + 1 < slab_count)
        def _():
            pass_x(slab + 1)

        pass_core(slab)
        whole_slab(slab)
        project(slab)
        fadings = []
        for block in range(block_count):
            rows = slice(block * GROUP, (block + 1) * GROUP)
            decay = decay_ref[chunk, :, rows]
            across = jnp.dot(decay, upper, precision=lax.Precision.HIGHEST, preferred_element_type=F32)
            down = lax.dot_general(
                lower,
                decay,
                (((1,), (1,)), ((), ())),
                precision=lax.Precision.HIGHEST,
                preferred_element_type=F32,
            )
            down_decay = lax.dot_general(
                unit,
                decay,
                (((1,), (1,)), ((), ())),
                precision=lax.Precision.HIGHEST,
                preferred_element_type=F32,
            )
            closing = down[GROUP - 1 : GROUP, :]
            scale = jnp.exp(closing - down) * (-down_decay)
            fading = jnp.exp(closing)
            grown = jnp.exp(down)
            fades = []
            for pair in range(head_count // 2):
                lanes = slice(pair * GROUP, (pair + 1) * GROUP)
                x_pair = mixed[rows, lanes]
                parts = []
                for head in (2 * pair, 2 * pair + 1):
                    gap = down[:, head : head + 1] - across[head : head + 1, :]
                    weights = (
                        scores[block]
                        * jnp.exp(jnp.minimum(gap, 0.0))
                        * (-decay[head : head + 1, :])
                    ).astype(BF16)
                    parts.append(jnp.dot(weights, x_pair, preferred_element_type=F32))
                x_wide = x_pair.astype(F32)
                intra[rows, lanes] = (
                    jnp.where(first_head, parts[0], parts[1])
                    + lane_ref[chunk, 0:1, lanes] * x_wide
                )
                scaled = (both(scale, pair) * x_wide).astype(BF16)
                block_states[block, :, lanes] = jnp.dot(
                    b_turned[block], scaled, preferred_element_type=F32
                )
                expanded[rows, lanes] = both(grown, pair)
                fades.append(both(fading, pair))
            fadings.append(jnp.concatenate(fades, axis=1))

        @pl.when(seq > 0)
        def _():
            state_copy(chunk).wait_recv()

        @pl.when(seq == 0)
        def _():
            arriving_state[chunk] = jnp.zeros(arriving_state.shape[1:], F32)

        state = arriving_state[chunk]
        for block in range(block_count):
            entering_half[block] = state.astype(BF16)
            state = fadings[block] * state + block_states[block]
        leaving_state[chunk] = state

        @pl.when(seq < seq_count - 1)
        def _():
            state_copy(chunk).start()

        for block in range(block_count):
            rows = slice(block * GROUP, (block + 1) * GROUP)
            inter = jnp.dot(c_held[block], entering_half[block], preferred_element_type=F32)
            ssm = intra[rows, :] + inter * expanded[rows, :]
            square = ssm * ssm
            high = square.astype(BF16)
            low = (square - high.astype(F32)).astype(BF16)
            for pair in range(head_count // 2):
                lanes = slice(pair * GROUP, (pair + 1) * GROUP)
                total = jnp.dot(
                    jnp.concatenate([high[:, lanes], low[:, lanes]], axis=1),
                    same_head_twice,
                    preferred_element_type=F32,
                )
                head_scale = lax.rsqrt(total * (1.0 / head_width) + 1e-05)
                normalized[rows, lanes] = (
                    ssm[:, lanes] * head_scale * lane_ref[chunk, 1:2, lanes]
                ).astype(BF16)
        picked[chunk] = jnp.dot(choice, normalized[...], preferred_element_type=F32).astype(BF16)
        for k in range(1, seq_count):
            target = (seq + k) % seq_count
            pltpu.make_async_remote_copy(
                src_ref=picked.at[chunk, pl.ds(pl.multiple_of(target * share, share), share)],
                dst_ref=result_ref.at[seq, :, out_columns(chunk)],
                send_sem=out_send.at[k - 1],
                recv_sem=out_recv.at[k - 1],
                device_id=(dp, target),
                device_id_type=MESH,
            ).start()
        pltpu.make_async_copy(
            picked.at[chunk, pl.ds(pl.multiple_of(seq * share, share), share)],
            result_ref.at[seq, :, out_columns(chunk)],
            own_sem,
        ).start()
        return carry

    lax.fori_loop(0, chunk_count, work, 0)

    for k in range(1, seq_count):
        source = (seq + seq_count - k) % seq_count
        whole = pltpu.make_async_remote_copy(
            src_ref=result_ref.at[source],
            dst_ref=result_ref.at[source],
            send_sem=out_send.at[k - 1],
            recv_sem=out_recv.at[k - 1],
            device_id=(dp, (seq + k) % seq_count),
            device_id_type=MESH,
        )
        whole.wait_recv()
        whole.wait_send()
    pltpu.make_async_copy(result_ref.at[seq], result_ref.at[seq], own_sem).wait()

    def settle(slab, carry):
        for k in range(1, z_count):
            z_copy(slab, k, z).wait_send()
        for k in range(1, x_count):
            x_copy(slab, k, x).wait_send()
        if core_count > 1:
            core_copy(slab, core).wait_send()
        return carry

    lax.fori_loop(0, slab_count, settle, 0)

    @pl.when(seq < seq_count - 1)
    def _():
        halo_copy.wait_send()

        def state_settle(chunk, carry):
            state_copy(chunk).wait_send()
            return carry

        lax.fori_loop(0, chunk_count, state_settle, 0)


def interleave_kernel(frame_count, arrived_ref, out_ref):
    rows = arrived_ref.shape[0]
    share = rows // frame_count
    row = lax.broadcasted_iota(jnp.int32, (rows, rows), 0)
    column = lax.broadcasted_iota(jnp.int32, (rows, rows), 1)
    choice = jnp.where(
        column == (row % frame_count) * share + row // frame_count, 1.0, 0.0
    ).astype(BF16)
    out_ref[...] = jnp.dot(choice, arrived_ref[...], preferred_element_type=F32).astype(BF16)


def on_device(
    sizes, tokens, in_gain, in_weight, conv_weight, conv_bias, log_decay, skip, out_gain, scan_order
):
    z_count, x_count, core_count, seq_count = sizes
    token_count, width = tokens.shape[1:]
    own_rows, channels = in_weight.shape
    heads = log_decay.shape[1]
    inner = out_gain.shape[0]
    head_width = inner // heads
    chunk_count = inner // CHUNK
    slab_count = chunk_count + 1
    per_chunk = heads // chunk_count
    taps = conv_weight.shape[0]
    positions = scan_order.shape[0]
    share = positions // seq_count
    assert token_count == positions and channels == inner + 2 * GROUP and per_chunk == 4

    def by_slab(rows):
        split = rows.reshape(rows.shape[0], slab_count, CHUNK).transpose(1, 0, 2)
        return jnp.concatenate([split[-1:], split[:-1]], axis=0)

    decay = log_decay[0].reshape(chunk_count, per_chunk, token_count)
    decay = jnp.pad(decay, ((0, 0), (0, 8 - per_chunk), (0, 0)))
    lane_skip = jnp.repeat(skip, head_width).reshape(chunk_count, 1, CHUNK)
    lane_gain = out_gain.reshape(chunk_count, 1, CHUNK)
    vmem = pl.BlockSpec(memory_space=pltpu.VMEM)
    hops = max(z_count - 1, 1), max(x_count - 1, 1), max(seq_count - 1, 1)
    arrived = pl.pallas_call(
        functools.partial(fused_kernel, sizes + (head_width,)),
        out_shape=jax.ShapeDtypeStruct((seq_count, share, inner), BF16),
        in_specs=[vmem] * 8,
        out_specs=pl.BlockSpec(memory_space=pl.ANY),
        scratch_shapes=[
            pltpu.VMEM(
                (slab_count, z_count, x_count, core_count, own_rows // core_count, CHUNK), BF16
            ),
            pltpu.VMEM((HALO + token_count, width), BF16),
            pltpu.VMEM((HALO + token_count, CHUNK), F32),
            pltpu.VMEM((token_count, CHUNK), BF16),
            pltpu.VMEM((token_count // GROUP, GROUP, GROUP), BF16),
            pltpu.VMEM((token_count // GROUP, GROUP, GROUP), BF16),
            pltpu.VMEM((token_count // GROUP, GROUP, GROUP), F32),
            pltpu.VMEM((token_count // GROUP, GROUP, CHUNK), F32),
            pltpu.VMEM((token_count // GROUP, GROUP, CHUNK), BF16),
            pltpu.VMEM((token_count, CHUNK), F32),
            pltpu.VMEM((token_count, CHUNK), F32),
            pltpu.VMEM((chunk_count, GROUP, CHUNK), F32),
            pltpu.VMEM((chunk_count, GROUP, CHUNK), F32),
            pltpu.VMEM((token_count, CHUNK), BF16),
            pltpu.VMEM((chunk_count, positions, CHUNK), BF16),
            pltpu.SemaphoreType.DMA((slab_count, hops[0])),
            pltpu.SemaphoreType.DMA((slab_count, hops[0])),
            pltpu.SemaphoreType.DMA((slab_count, hops[1])),
            pltpu.SemaphoreType.DMA((slab_count, hops[1])),
            pltpu.SemaphoreType.DMA((slab_count,)),
            pltpu.SemaphoreType.DMA((slab_count,)),
            pltpu.SemaphoreType.DMA,
            pltpu.SemaphoreType.DMA,
            pltpu.SemaphoreType.DMA((chunk_count,)),
            pltpu.SemaphoreType.DMA((chunk_count,)),
            pltpu.SemaphoreType.DMA((hops[2],)),
            pltpu.SemaphoreType.DMA((hops[2],)),
            pltpu.SemaphoreType.DMA,
        ],
        compiler_params=pltpu.CompilerParams(
            collective_id=0, has_side_effects=True, vmem_limit_bytes=52 * 1024 * 1024
        ),
        name="projected_scan",
    )(
        tokens[0],
        in_gain.reshape(1, width),
        in_weight,
        by_slab(conv_weight),
        by_slab(conv_bias.reshape(1, channels)),
        decay,
        jnp.concatenate([lane_skip, lane_gain], axis=1),
        scan_order.reshape(positions, 1),
    )
    columns = min(512, inner)
    out = pl.pallas_call(
        functools.partial(interleave_kernel, seq_count),
        out_shape=jax.ShapeDtypeStruct((token_count, inner), BF16),
        grid=(inner // columns,),
        in_specs=[pl.BlockSpec((token_count, columns), lambda i: (0, i))],
        out_specs=pl.BlockSpec((token_count, columns), lambda i: (0, i)),
        name="frames_within_positions",
    )(arrived.reshape(token_count, inner))
    return out[None]


def solution(mesh):
    dp_count, seq_count = mesh.shape["dp"], mesh.shape["seq"]
    x_count = 2 ** (int(math.log2(dp_count)) // 2)
    while dp_count % x_count:
        x_count //= 2
    sizes = (dp_count // x_count, x_count, 2 if seq_count % 2 == 0 else 1, seq_count)
    in_specs = (
        P("dp", "seq", None),
        P(),
        P("dp", None),
        P(),
        P(),
        P("dp", None, "seq"),
        P(),
        P(),
        P(),
    )
    return jax.shard_map(
        functools.partial(on_device, sizes),
        mesh=mesh,
        in_specs=in_specs,
        out_specs=P("dp", "seq", None),
        check_vma=False,
    )
```

time: 274 us -> 117 us (0.43)
  waiting for transfers between devices: 123 us -> 0 us
  Pallas kernels: 0 us -> 107 us
  local copies, waits for them, and re-layouts: 48.9 us -> 7.39 us
  blocking collectives: 35.8 us -> 0 us
  matrix products: 24.3 us -> 0 us
  other arithmetic: 22.3 us -> 0.74 us
  between operations: 14.2 us -> 0.04 us
    all_gather x3 -> x0, waiting for transfers between devices: 123 us -> none  [the longest x1 62.4 us: project(): lax.all_gather(full_slab, 'seq', axis=1, tiled=True)]
    pallas_call x0 -> x2, Pallas kernels: none -> 107 us  [the longest x1 102 us: on_device(): pl.pallas_call(functools.partial(fused_kernel, sizes + (head_width,)), ou...]
    all_to_all x1 -> x0, blocking collectives: 30.7 us -> none  [on_device(): lax.all_to_all(outgoing, 'seq', split_axis=0, concat_axis=2, tiled=True)]
    dot_general x17 -> x0, matrix products: 24.3 us -> none  [the longest x1 9.08 us: project(): jnp.dot(operand, lax.all_gather(full_slab, 'seq', axis=1, tiled=True), pr...]
    convert_element_type x3 -> x0, other arithmetic: 10.5 us -> none  [the longest x1 4.63 us: on_device(): (ssm_out * head_scale * out_gain.reshape(HALF_HEADS, HEADDIM)[None]).asty...]
    mul x5 -> x0, local copies, waits for them, and re-layouts: 9.44 us -> none  [the longest x2 7.96 us: on_device(): ssm_out * head_scale * out_gain.reshape(HALF_HEADS, HEADDIM)[None]]
    unnamed x96 -> x4, local copies, waits for them, and re-layouts: 10.7 us -> 1.96 us
    convert_element_type x1 -> x0, local copies, waits for them, and re-layouts: 5.45 us -> none  [on_device(): x_heads.astype(jnp.float32)]
  transfers between devices with their start and end apart: 4 -> 0, of which waited for: 3 -> 0; matrix products, arithmetic and copies ran while one was open for 10% -> 0% of each run, Pallas kernels for 0% -> 0%
where the time goes in v1:
time: 117 us; the launch traced here: 115 us
  Pallas kernels  107 us (91%)
  local copies, waits for them, and re-layouts  7.39 us (6%)
    pallas_call x1, Pallas kernels, on_device(): pl.pallas_call(functools.partial(fused_kernel, sizes + (head_width,)), ou...  102 us
    pallas_call x1, Pallas kernels, on_device(): pl.pallas_call(functools.partial(interleave_kernel, seq_count), out_shape...  4.6 us
    slice x4, local copies, waits for them, and re-layouts, by_slab(): return jnp.concatenate([split[-1:], split[:-1]], axis=0)  2.84 us

profile of v1, /device:TPU:25, one launch (start us, length us, event | category | flops | bytes accessed | tf_op | source)
XLA Modules:
  0.0 114.9 jit_solution(4513123930333646038)
XLA Ops:
  0.0 0.7 slice.28
  0.7 0.7 slice.32
  1.4 0.7 broadcast_in_dim.10
  2.1 0.7 slice.30
  2.8 0.1 broadcast_in_dim.11
  2.9 0.1 broadcast_in_dim.12
  3.0 0.7 pad_maximum_fusion.1.lane_ref
  3.7 0.8 slice.33
  4.5 0.9 reshape_squeeze.3
  5.4 0.8 copy.10.order_ref
  6.2 0.0 copy-start
  6.2 1.3 %copy-done = bf16[256,2304]{1,0:T(8,128)(2,1)S(1)} copy-done((bf16[256,2304]{1,0:T(8,128)(2,1)S(1)}, bf16[256,2304]{1,0:T(8,128)(2,1)}, u32[]{:S(2)}) %copy-start) | copy-done | bytes 1179672
  7.5 0.0 copy-start.1
  7.5 0.7 copy-done.1
  8.2 102.2 %projected_scan.1 = bf16[4,128,2048]{2,1,0:T(8,128)(2,1)} custom-call(bf16[512,2048]{1,0:T(8,128)(2,1)} %bitcast.13, f32[1,2048]{1,0:T(1,128)S(1)} %bitcast.11, bf16[256,2304]{1,0:T(8,128)(2,1)S(1)} %copy-done, f32[9,4,256]{2,1,0:T(4,128)S(1)} %pad_maximum_fusion.conv_weight_ref, f32[9,1,256]{2,1,0:T(1,128)S(1)} %pad_maximum_fusion.2.conv_bias_ref, ...), custom_call_target="tpu_custom_call" | custom-call | tf_op jit(solution)/shard_map/projected_scan/pallas_call | solution.py:420
  110.4 4.6 %frames_within_positions.1 = bf16[512,2048]{1,0:T(8,128)(2,1)} custom-call(bf16[512,2048]{1,0:T(8,128)(2,1)} %bitcast.12), custom_call_target="tpu_custom_call" | custom-call | tf_op jit(solution)/shard_map/frames_within_positions/pallas_call | solution.py:472
  (3 shorter events, 0.0 us)
Async XLA Ops:
  6.2 1.3 %copy-start = (bf16[256,2304]{1,0:T(8,128)(2,1)S(1)}, bf16[256,2304]{1,0:T(8,128)(2,1)}, u32[]{:S(2)}) copy-start(bf16[256,2304]{1,0:T(8,128)(2,1)} %weight_ref.1) | copy-start | bytes 3538948
  7.5 0.7 copy-start.1

commit v2 on v1

--- a/solution.py
+++ b/solution.py
@@ -11,6 +11,7 @@
 GROUP = 128
 CHUNK = 256
 HALO = 16
+WINDOW = 3
 BF16 = jnp.bfloat16
 F32 = jnp.float32
 MESH = pl.DeviceIdType.MESH
@@ -18,17 +19,24 @@
 
 def fused_kernel(
     sizes,
-    tokens_ref,
+    tokens_hbm,
     gain_ref,
-    weight_ref,
+    weight_hbm,
     conv_weight_ref,
     conv_bias_ref,
     decay_ref,
-    lane_ref,
+    skip_ref,
+    out_gain_ref,
     order_ref,
     result_ref,
+    tokens_ref,
     slabs,
     normed,
+    choice,
+    down_held,
+    down_decay_held,
+    across_held,
+    decay_held,
     projected,
     mixed,
     b_turned,
@@ -55,6 +63,8 @@
     out_send,
     out_recv,
     own_sem,
+    token_sem,
+    weight_sem,
 ):
     z_count, x_count, core_count, seq_count, head_width = sizes
     head_count = CHUNK // head_width
@@ -69,7 +79,7 @@
     chunk_count = slab_count - 1
     token_count, width = tokens_ref.shape
     block_count = token_count // GROUP
-    positions = order_ref.shape[0]
+    positions = order_ref.shape[1]
     share = positions // seq_count
 
     partners = [(((z + k) % z_count) * x_count + x, seq) for k in range(1, z_count)]
@@ -80,9 +90,25 @@
         pl.semaphore_signal(barrier, inc=1, device_id=partner, device_id_type=MESH)
 
     own_rows = pl.ds(pl.multiple_of(core * half, half), half)
+
+    def load_weight(slab):
+        first = chunk_count * CHUNK if slab == 0 else (slab - 1) * CHUNK
+        return pltpu.make_async_copy(
+            weight_hbm.at[own_rows, first : first + CHUNK],
+            slabs.at[slab, z, x, core],
+            weight_sem.at[slab],
+        )
+
+    def load_tokens(block):
+        rows = slice(block * GROUP, (block + 1) * GROUP)
+        return pltpu.make_async_copy(tokens_hbm.at[rows], tokens_ref.at[rows], token_sem.at[block])
+
     for slab in range(slab_count):
-        first = chunk_count * CHUNK if slab == 0 else (slab - 1) * CHUNK
-        slabs[slab, z, x, core] = weight_ref[own_rows, first : first + CHUNK]
+        load_weight(slab).start()
+    for block in range(block_count):
+        load_tokens(block).start()
+    for slab in range(slab_count):
+        load_weight(slab).wait()
     pl.semaphore_wait(barrier, len(partners))
 
     def z_copy(slab, k, source):
@@ -95,10 +121,11 @@
             device_id_type=MESH,
         )
 
-    def x_copy(slab, k, source):
+    def x_copy(slab, k, source, row):
+        piece = slabs.at[slab, row, source, core]
         return pltpu.make_async_remote_copy(
-            src_ref=slabs.at[slab, :, source, core],
-            dst_ref=slabs.at[slab, :, source, core],
+            src_ref=piece,
+            dst_ref=piece,
             send_sem=x_send.at[slab, k - 1],
             recv_sem=x_recv.at[slab, k - 1],
             device_id=(z * x_count + (x + k) % x_count, seq),
@@ -115,19 +142,31 @@
             device_id_type=MESH,
         )
 
-    for slab in range(slab_count):
+    def send_own(slab):
         for k in range(1, z_count):
             z_copy(slab, k, z).start()
+        for k in range(1, x_count):
+            x_copy(slab, k, x, z).start()
 
     def pass_x(slab):
         for k in range(1, z_count):
-            z_copy(slab, k, (z + z_count - k) % z_count).wait_recv()
-        for k in range(1, x_count):
-            x_copy(slab, k, x).start()
+            row = (z + z_count - k) % z_count
+            z_copy(slab, k, row).wait_recv()
+            for kx in range(1, x_count):
+                x_copy(slab, kx, x, row).start()
+
+        if isinstance(slab, int):
+            if slab + WINDOW < slab_count:
+                send_own(slab + WINDOW)
+        else:
+
+            @pl.when(slab + WINDOW < slab_count)
+            def _():
+                send_own(slab + WINDOW)
 
     def pass_core(slab):
         for k in range(1, x_count):
-            x_copy(slab, k, (x + x_count - k) % x_count).wait_recv()
+            x_copy(slab, k, (x + x_count - k) % x_count, slice(None)).wait_recv()
         if core_count > 1:
             core_copy(slab, core).start()
 
@@ -135,7 +174,11 @@
         if core_count > 1:
             core_copy(slab, (core + 1) % core_count).wait_recv()
 
+    for slab in range(min(WINDOW, slab_count)):
+        send_own(slab)
+
     for block in range(block_count):
+        load_tokens(block).wait()
         rows = tokens_ref[block * GROUP : (block + 1) * GROUP, :].astype(F32)
         inverse = lax.rsqrt(jnp.mean(rows * rows, axis=1, keepdims=True) + 1e-05)
         normed[HALO + block * GROUP : HALO + (block + 1) * GROUP, :] = (
@@ -169,17 +212,18 @@
     same_head = jnp.where(row_at // head_width == column_at // head_width, 1.0, 0.0).astype(BF16)
     same_head_twice = jnp.concatenate([same_head, same_head], axis=0)
 
-    def project(slab):
+    def project(slab, first_column):
+        columns = pl.ds(first_column, CHUNK)
         matrix = slabs[slab].reshape(width, CHUNK)
         projected[...] = (
             jnp.dot(normed[...], matrix, preferred_element_type=F32).astype(BF16).astype(F32)
         )
-        taps = conv_weight_ref.shape[1]
+        taps = conv_weight_ref.shape[0]
         for block in range(block_count):
-            total = conv_bias_ref[slab]
+            total = conv_bias_ref[:, columns]
             for tap in range(taps):
                 first = HALO + block * GROUP + tap - (taps - 1)
-                total = total + conv_weight_ref[slab, tap : tap + 1, :] * projected[
+                total = total + conv_weight_ref[tap : tap + 1, columns] * projected[
                     first : first + GROUP, :
                 ]
             mixed[block * GROUP : (block + 1) * GROUP, :] = (total / (1.0 + jnp.exp(-total))).astype(
@@ -192,15 +236,39 @@
         )
 
     pass_x(0)
+    for block in range(block_count):
+        rows = slice(block * GROUP, (block + 1) * GROUP)
+        decay = decay_ref[:, rows]
+        across = jnp.dot(decay, upper, precision=lax.Precision.HIGHEST, preferred_element_type=F32)
+        turned = (((1,), (1,)), ((), ()))
+        down = lax.dot_general(
+            lower, decay, turned, precision=lax.Precision.HIGHEST, preferred_element_type=F32
+        )
+        down_decay = lax.dot_general(
+            unit, decay, turned, precision=lax.Precision.HIGHEST, preferred_element_type=F32
+        )
+        for chunk in range(chunk_count):
+            heads = slice(chunk * head_count, (chunk + 1) * head_count)
+            down_held[chunk, rows, :head_count] = down[:, heads]
+            down_decay_held[chunk, rows, :head_count] = down_decay[:, heads]
+            across_held[chunk, :head_count, rows] = across[heads, :]
+            decay_held[chunk, :head_count, rows] = decay[heads, :]
+    pass_core(0)
     pass_x(1)
-    pass_core(0)
+    choice[...] = jnp.transpose(
+        jnp.where(
+            lax.broadcasted_iota(jnp.int32, (positions, positions), 0) == order_ref[...], 1.0, 0.0
+        ).astype(F32)
+    ).astype(BF16)
 
     @pl.when(seq > 0)
     def _():
         halo_copy.wait_recv()
 
     whole_slab(0)
-    project(0)
+    project(0, chunk_count * CHUNK)
+    pass_x(2)
+    pass_core(1)
     for block in range(block_count):
         rows = slice(block * GROUP, (block + 1) * GROUP)
         b_block = mixed[rows, :GROUP]
@@ -210,11 +278,6 @@
         scores[block] = jnp.where(
             causal, jnp.dot(c_block, b_turned[block], preferred_element_type=F32), 0.0
         )
-    order = order_ref[...]
-    choice = jnp.where(
-        lax.broadcasted_iota(jnp.int32, (positions, positions), 1) == order, 1.0, 0.0
-    ).astype(BF16)
-
     def state_copy(chunk):
         return pltpu.make_async_remote_copy(
             src_ref=leaving_state.at[chunk],
@@ -231,53 +294,51 @@
     def work(chunk, carry):
         slab = chunk + 1
 
-        @pl.when(slab + 1 < slab_count)
+        whole_slab(slab)
+        project(slab, pl.multiple_of(chunk * CHUNK, CHUNK))
+
+        @pl.when(slab + 2 < slab_count)
         def _():
-            pass_x(slab + 1)
-
-        pass_core(slab)
-        whole_slab(slab)
-        project(slab)
+            pass_x(slab + 2)
+
         fadings = []
         for block in range(block_count):
             rows = slice(block * GROUP, (block + 1) * GROUP)
-            decay = decay_ref[chunk, :, rows]
-            across = jnp.dot(decay, upper, precision=lax.Precision.HIGHEST, preferred_element_type=F32)
-            down = lax.dot_general(
-                lower,
-                decay,
-                (((1,), (1,)), ((), ())),
-                precision=lax.Precision.HIGHEST,
-                preferred_element_type=F32,
-            )
-            down_decay = lax.dot_general(
-                unit,
-                decay,
-                (((1,), (1,)), ((), ())),
-                precision=lax.Precision.HIGHEST,
-                preferred_element_type=F32,
-            )
+            decay = decay_held[chunk, :head_count, rows]
+            across = across_held[chunk, :head_count, rows]
+            down = down_held[chunk, rows, :head_count]
             closing = down[GROUP - 1 : GROUP, :]
-            scale = jnp.exp(closing - down) * (-down_decay)
+            scale = jnp.exp(closing - down) * (-down_decay_held[chunk, rows, :head_count])
             fading = jnp.exp(closing)
             grown = jnp.exp(down)
             fades = []
             for pair in range(head_count // 2):
                 lanes = slice(pair * GROUP, (pair + 1) * GROUP)
                 x_pair = mixed[rows, lanes]
-                parts = []
+                x_wide = x_pair.astype(F32)
+                weights = []
                 for head in (2 * pair, 2 * pair + 1):
                     gap = down[:, head : head + 1] - across[head : head + 1, :]
-                    weights = (
-                        scores[block]
-                        * jnp.exp(jnp.minimum(gap, 0.0))
-                        * (-decay[head : head + 1, :])
-                    ).astype(BF16)
-                    parts.append(jnp.dot(weights, x_pair, preferred_element_type=F32))
-                x_wide = x_pair.astype(F32)
+                    weights.append(
+                        (
+                            scores[block]
+                            * jnp.exp(jnp.minimum(gap, 0.0))
+                            * (-decay[head : head + 1, :])
+                        ).astype(BF16)
+                    )
+                x_apart = jnp.concatenate(
+                    [jnp.where(first_head, x_wide, 0.0), jnp.where(first_head, 0.0, x_wide)], axis=0
+                ).astype(BF16)
+                skips = jnp.where(
+                    first_head,
+                    skip_ref[chunk * head_count + 2 * pair],
+                    skip_ref[chunk * head_count + 2 * pair + 1],
+                )
                 intra[rows, lanes] = (
-                    jnp.where(first_head, parts[0], parts[1])
-                    + lane_ref[chunk, 0:1, lanes] * x_wide
+                    jnp.dot(
+                        jnp.concatenate(weights, axis=1), x_apart, preferred_element_type=F32
+                    )
+                    + skips * x_wide
                 )
                 scaled = (both(scale, pair) * x_wide).astype(BF16)
                 block_states[block, :, lanes] = jnp.dot(
@@ -287,6 +348,10 @@
                 fades.append(both(fading, pair))
             fadings.append(jnp.concatenate(fades, axis=1))
 
+        @pl.when(slab + 1 < slab_count)
+        def _():
+            pass_core(slab + 1)
+
         @pl.when(seq > 0)
         def _():
             state_copy(chunk).wait_recv()
@@ -305,6 +370,7 @@
         def _():
             state_copy(chunk).start()
 
+        gains = out_gain_ref[:, out_columns(chunk)]
         for block in range(block_count):
             rows = slice(block * GROUP, (block + 1) * GROUP)
             inter = jnp.dot(c_held[block], entering_half[block], preferred_element_type=F32)
@@ -321,9 +387,9 @@
                 )
                 head_scale = lax.rsqrt(total * (1.0 / head_width) + 1e-05)
                 normalized[rows, lanes] = (
-                    ssm[:, lanes] * head_scale * lane_ref[chunk, 1:2, lanes]
+                    ssm[:, lanes] * head_scale * gains[:, lanes]
                 ).astype(BF16)
-        picked[chunk] = jnp.dot(choice, normalized[...], preferred_element_type=F32).astype(BF16)
+        picked[chunk] = jnp.dot(choice[...], normalized[...], preferred_element_type=F32).astype(BF16)
         for k in range(1, seq_count):
             target = (seq + k) % seq_count
             pltpu.make_async_remote_copy(
@@ -361,7 +427,7 @@
         for k in range(1, z_count):
             z_copy(slab, k, z).wait_send()
         for k in range(1, x_count):
-            x_copy(slab, k, x).wait_send()
+            x_copy(slab, k, x, slice(None)).wait_send()
         if core_count > 1:
             core_copy(slab, core).wait_send()
         return carry
@@ -380,14 +446,20 @@
 
 
 def interleave_kernel(frame_count, arrived_ref, out_ref):
-    rows = arrived_ref.shape[0]
-    share = rows // frame_count
+    share = arrived_ref.shape[1]
+    step = min(share, max(GROUP // frame_count, 16))
+    rows = step * frame_count
     row = lax.broadcasted_iota(jnp.int32, (rows, rows), 0)
     column = lax.broadcasted_iota(jnp.int32, (rows, rows), 1)
-    choice = jnp.where(
-        column == (row % frame_count) * share + row // frame_count, 1.0, 0.0
-    ).astype(BF16)
-    out_ref[...] = jnp.dot(choice, arrived_ref[...], preferred_element_type=F32).astype(BF16)
+    frame = column // step
+    choice = jnp.where(row == (column - frame * step) * frame_count + frame, 1.0, 0.0).astype(BF16)
+    for first in range(0, share, step):
+        block = jnp.concatenate(
+            [arrived_ref[f, first : first + step, :] for f in range(frame_count)], axis=0
+        )
+        out_ref[first * frame_count : first * frame_count + rows, :] = jnp.dot(
+            choice, block, preferred_element_type=F32
+        ).astype(BF16)
 
 
 def on_device(
@@ -407,26 +479,27 @@
     share = positions // seq_count
     assert token_count == positions and channels == inner + 2 * GROUP and per_chunk == 4
 
-    def by_slab(rows):
-        split = rows.reshape(rows.shape[0], slab_count, CHUNK).transpose(1, 0, 2)
-        return jnp.concatenate([split[-1:], split[:-1]], axis=0)
-
-    decay = log_decay[0].reshape(chunk_count, per_chunk, token_count)
-    decay = jnp.pad(decay, ((0, 0), (0, 8 - per_chunk), (0, 0)))
-    lane_skip = jnp.repeat(skip, head_width).reshape(chunk_count, 1, CHUNK)
-    lane_gain = out_gain.reshape(chunk_count, 1, CHUNK)
     vmem = pl.BlockSpec(memory_space=pltpu.VMEM)
+    smem = pl.BlockSpec(memory_space=pltpu.SMEM)
+    hbm = pl.BlockSpec(memory_space=pl.ANY)
+    block_count = token_count // GROUP
     hops = max(z_count - 1, 1), max(x_count - 1, 1), max(seq_count - 1, 1)
     arrived = pl.pallas_call(
         functools.partial(fused_kernel, sizes + (head_width,)),
         out_shape=jax.ShapeDtypeStruct((seq_count, share, inner), BF16),
-        in_specs=[vmem] * 8,
+        in_specs=[hbm, vmem, hbm, vmem, vmem, vmem, smem, vmem, vmem],
         out_specs=pl.BlockSpec(memory_space=pl.ANY),
         scratch_shapes=[
+            pltpu.VMEM((token_count, width), BF16),
             pltpu.VMEM(
                 (slab_count, z_count, x_count, core_count, own_rows // core_count, CHUNK), BF16
             ),
             pltpu.VMEM((HALO + token_count, width), BF16),
+            pltpu.VMEM((positions, positions), BF16),
+            pltpu.VMEM((chunk_count, token_count, GROUP), F32),
+            pltpu.VMEM((chunk_count, token_count, GROUP), F32),
+            pltpu.VMEM((chunk_count, 8, token_count), F32),
+            pltpu.VMEM((chunk_count, 8, token_count), F32),
             pltpu.VMEM((HALO + token_count, CHUNK), F32),
             pltpu.VMEM((token_count, CHUNK), BF16),
             pltpu.VMEM((token_count // GROUP, GROUP, GROUP), BF16),
@@ -453,6 +526,8 @@
             pltpu.SemaphoreType.DMA((hops[2],)),
             pltpu.SemaphoreType.DMA((hops[2],)),
             pltpu.SemaphoreType.DMA,
+            pltpu.SemaphoreType.DMA((block_count,)),
+            pltpu.SemaphoreType.DMA((slab_count,)),
         ],
         compiler_params=pltpu.CompilerParams(
             collective_id=0, has_side_effects=True, vmem_limit_bytes=52 * 1024 * 1024
@@ -462,21 +537,22 @@
         tokens[0],
         in_gain.reshape(1, width),
         in_weight,
-        by_slab(conv_weight),
-        by_slab(conv_bias.reshape(1, channels)),
-        decay,
-        jnp.concatenate([lane_skip, lane_gain], axis=1),
-        scan_order.reshape(positions, 1),
+        conv_weight,
+        conv_bias.reshape(1, channels),
+        log_decay[0],
+        skip,
+        out_gain.reshape(1, inner),
+        scan_order.reshape(1, positions),
     )
     columns = min(512, inner)
     out = pl.pallas_call(
         functools.partial(interleave_kernel, seq_count),
         out_shape=jax.ShapeDtypeStruct((token_count, inner), BF16),
         grid=(inner // columns,),
-        in_specs=[pl.BlockSpec((token_count, columns), lambda i: (0, i))],
+        in_specs=[pl.BlockSpec((seq_count, share, columns), lambda i: (0, 0, i))],
         out_specs=pl.BlockSpec((token_count, columns), lambda i: (0, i)),
         name="frames_within_positions",
-    )(arrived.reshape(token_count, inner))
+    )(arrived)
     return out[None]
 
 

time: 117 us -> 99.8 us (0.85); the launches traced: 115 us -> 99.3 us
  Pallas kernels: 107 us -> 93 us
    pallas_call x1, Pallas kernels: 102 us -> 88.7 us  [on_device(): pl.pallas_call(functools.partial(fused_kernel, sizes + (head_width,)), ou...]
    unnamed x4 -> x14, local copies, waits for them, and re-layouts: 1.96 us -> 5.6 us
    slice x4 -> x0, local copies, waits for them, and re-layouts: 2.84 us -> none  [by_slab(): return jnp.concatenate([split[-1:], split[:-1]], axis=0)]
where the time goes in v2:
time: 99.8 us; the launch traced here: 99.3 us
  Pallas kernels  93 us (93%)
  local copies, waits for them, and re-layouts  6.32 us (6%)
    pallas_call x1, Pallas kernels, on_device(): pl.pallas_call(functools.partial(fused_kernel, sizes + (head_width,)), ou...  88.7 us
    unnamed x14, local copies, waits for them, and re-layouts  5.6 us
    pallas_call x1, Pallas kernels, on_device(): pl.pallas_call(functools.partial(interleave_kernel, seq_count), out_shape...  4.28 us

profile of v2, /device:TPU:25, one launch (start us, length us, event | category | flops | bytes accessed | tf_op | source)
XLA Modules:
  0.0 99.3 jit_solution(5976835594525035632)
XLA Ops:
  0.0 0.7 reshape.13.conv_bias_ref
  0.7 0.0 copy-start
  0.7 1.3 %copy-done = bf16[256,2304]{1,0:T(8,128)(2,1)S(1)} copy-done((bf16[256,2304]{1,0:T(8,128)(2,1)S(1)}, bf16[256,2304]{1,0:T(8,128)(2,1)}, u32[]{:S(2)}) %copy-start) | copy-done | bytes 1179672
  2.0 0.0 copy-start.1
  2.0 0.8 copy-done.1
  2.8 0.0 copy-start.2
  2.8 0.8 copy-done.2
  3.6 0.0 copy-start.3
  3.6 0.7 copy-done.3
  4.3 0.0 copy-start.4
  4.3 0.7 copy-done.4
  5.0 0.0 copy-start.5
  5.0 0.7 copy-done.5
  5.7 0.0 copy-start.6
  5.7 0.7 copy-done.6
  6.3 88.7 %projected_scan.1.arrived_ref = bf16[4,128,2048]{2,1,0:T(8,128)(2,1)} custom-call(bf16[512,2048]{1,0:T(8,128)(2,1)} %bitcast.10, f32[1,2048]{1,0:T(1,128)S(1)} %bitcast.7, bf16[256,2304]{1,0:T(8,128)(2,1)S(1)} %copy-done, f32[4,2304]{1,0:T(4,128)S(1)} %copy-done.2, f32[1,2304]{1,0:T(1,128)S(1)} %reshape.13.conv_bias_ref, f32[32,512]{1,0:T(8,128)S(1)} %bitcast.6, ...), custom_call_target="tpu_custom_call" | custom-call | tf_op jit(solution)/shard_map/projected_scan/pallas_call | solution.py:487
  95.0 4.3 %frames_within_positions.1 = bf16[512,2048]{1,0:T(8,128)(2,1)} custom-call(bf16[4,128,2048]{2,1,0:T(8,128)(2,1)} %projected_scan.1.arrived_ref), custom_call_target="tpu_custom_call" | custom-call | tf_op jit(solution)/shard_map/frames_within_positions/pallas_call | solution.py:548
Async XLA Ops:
  0.7 1.3 %copy-start = (bf16[256,2304]{1,0:T(8,128)(2,1)S(1)}, bf16[256,2304]{1,0:T(8,128)(2,1)}, u32[]{:S(2)}) copy-start(bf16[256,2304]{1,0:T(8,128)(2,1)} %weight_hbm.1) | copy-start | bytes 3538948
  2.0 0.8 copy-start.1
  2.8 0.8 copy-start.2
  3.6 0.7 copy-start.3
  4.3 0.7 copy-start.4
  5.0 0.7 copy-start.5
  5.7 0.7 copy-start.6
